TPU v7x, 32 devices: a whole 2x2x4 slice. The times are simulated.
32 devices in a mesh: row: 8 (over y, x, core), col: 4 (over z).
Axes of the slice: x: 2, y: 2, z: 4, core: 2. Of those that a mesh axis runs over, the one named last changes fastest.
Arguments:
- front_init: float32 [16, 16, 2, 1024], P(None, None, None, 'row'), may hold values from -3 to 3
- green_hist: float32 [64, 16, 2, 1024], P('row', None, None, 'col'), may hold values from -0.125 to 0.125
- field_hist: float32 [64, 16, 2, 1024], P('row', None, None, 'col'), may hold values from -0.125 to 0.125
Outputs:
- front_final: float32 [16, 16, 2, 1024], P(None, None, None, 'row')
All inputs are finite; a program needn't handle non-finite values.
Results may differ from a plain program's by a relative error of at most 0.0001.
Values sent between devices are 32-bit elements; how exact they have to be, the bound alone decides.
A program may use at most 64 MiB of HBM per device.

v0:
```python
import jax
import jax.numpy as jnp
from jax import lax
from jax.sharding import PartitionSpec as P

ITERS = 2


STEP_WEIGHT = 0.5


def broadcast(x, axis, root):
    mine = lax.axis_index(axis) == root
    return lax.psum(jnp.where(mine, x, jnp.zeros_like(x)), axis)


def product(left, right):
    return jnp.dot(left, right, precision=lax.Precision.HIGHEST, preferred_element_type=jnp.float32)


def cubic_sigma(current):
    count, orbits, parts, length = current.shape
    swapped = current.reshape(count, orbits, parts, length // orbits, orbits)
    swapped = swapped.transpose(0, 4, 2, 3, 1).reshape(current.shape)
    real_part = current[:, :, 0, :]
    imag_part = current[:, :, 1, :]
    square_re = real_part * real_part - imag_part * imag_part
    square_im = 2.0 * real_part * imag_part
    other_re = swapped[:, :, 0, :]
    other_im = swapped[:, :, 1, :]
    sigma_re = square_re * other_re + square_im * other_im
    sigma_im = square_im * other_re - square_re * other_im
    return (sigma_re, sigma_im)


def collide(current, green_re, green_im, field_re, field_im):
    count, orbits, parts, length = current.shape
    sigma_re, sigma_im = cubic_sigma(current)
    sigma_re = sigma_re.reshape(count * orbits, length)
    sigma_im = sigma_im.reshape(count * orbits, length)
    front_re = current[:, :, 0, :].reshape(count * orbits, length)
    front_im = current[:, :, 1, :].reshape(count * orbits, length)
    image_re = (
        product(sigma_re, green_re)
        - product(sigma_im, green_im)
        + product(front_re, field_re)
        - product(front_im, field_im)
    )
    image_im = (
        product(sigma_re, green_im)
        + product(sigma_im, green_re)
        + product(front_re, field_im)
        + product(front_im, field_re)
    )
    image_re = image_re.reshape(count, orbits, -1)
    image_im = image_im.reshape(count, orbits, -1)
    return jnp.stack([image_re, image_im], axis=2)


def matrices(history):
    rows = history.shape[0] * history.shape[1]
    return (history[:, :, 0, :].reshape(rows, -1), history[:, :, 1, :].reshape(rows, -1))


def per_device(front_init, green_hist, field_hist):
    ratio = lax.axis_size("row") // lax.axis_size("col")
    row_place = lax.axis_index("row")
    owner_col = row_place // ratio
    width = front_init.shape[3]
    offset = row_place % ratio * width
    green_re, green_im = matrices(green_hist)
    field_re, field_im = matrices(field_hist)
    current = front_init
    for sweep in range(ITERS):
        partial_value = collide(current, green_re, green_im, field_re, field_im)
        totals = lax.psum(partial_value, "row")
        needed = lax.dynamic_slice_in_dim(totals, offset, width, 3)
        arrived = broadcast(needed, "col", owner_col)
        current = front_init + STEP_WEIGHT * arrived
    return current


def solution(mesh):
    in_specs = (
        P(None, None, None, "row"),
        P("row", None, None, "col"),
        P("row", None, None, "col"),
    )
    out_specs = P(None, None, None, "row")
    return jax.shard_map(
        per_device, mesh=mesh, in_specs=in_specs, out_specs=out_specs, check_vma=False
    )
```

profile of v0, /device:TPU:0, one launch (start us, length us, event | category | flops | bytes accessed | tf_op | source)
XLA Modules:
  0.0 226.5 jit_solution(1818639280756104975)
XLA Ops:
  6.5 1.3 fusion.1
  7.9 1.3 fusion
  9.2 2.1 reshape.40
  11.4 2.6 %copy.10 = f32[16,16,2,8,16]{1,3,2,4,0:T(8,128)S(1)} copy(f32[16,16,2,8,16]{4,3,2,1,0:T(8,128)} %reshape.40) | data formatting | bytes 524288 | tf_op jit(solution)/shard_map/reshape | solution.py:23
  14.0 0.9 reshape.41
  14.9 0.5 multiply_subtract_fusion.2
  17.9 0.4 convolution_add_fusion.7
  18.3 0.4 convolution_subtract_fusion.2
  18.9 1.3 pad_maximum_fusion
  20.3 57.3 %all-reduce.5.cloned.1.call-done = f32[16,16,2,256]{3,2,1,0:T(2,128)} async-done(((f32[16,16,2,256]{3,2,1,0:T(2,128)}), f32[16,16,2,256]{3,2,1,0:T(2,128)}) %all-reduce.5.cloned.1.call-update) | async-done | bytes 524304 | tf_op jit(solution)/shard_map/psum | solution.py:76
  77.6 1.8 dynamic-slice_select_fusion.1
  79.6 35.1 %all-reduce.7.cloned.1.call-done = f32[16,16,2,128]{3,2,1,0:T(2,128)} async-done(((f32[16,16,2,128]{3,2,1,0:T(2,128)}), f32[16,16,2,128]{3,2,1,0:T(2,128)}) %all-reduce.7.cloned.1.call-update) | async-done | bytes 262160 | tf_op jit(solution)/shard_map/psum | solution.py:14
  114.7 1.1 multiply_add_fusion.1
  115.8 2.1 reshape.42
  117.9 2.6 %copy.17 = f32[16,16,2,8,16]{4,3,2,1,0:T(8,128)S(1)} copy(f32[16,16,2,8,16]{1,3,2,4,0:T(8,128)} %bitcast.55) | data formatting | bytes 524288 | tf_op jit(solution)/shard_map/transpose | solution.py:24
  120.5 0.9 reshape.43
  121.4 0.5 multiply_subtract_fusion
  123.8 0.4 convolution_add_fusion.1
  124.2 0.4 convolution_subtract_fusion
  125.5 1.3 pad_maximum_fusion.1
  126.8 54.4 %all-reduce.9.cloned.1.call-done = f32[16,16,2,256]{3,2,1,0:T(2,128)} async-done(((f32[16,16,2,256]{3,2,1,0:T(2,128)}), f32[16,16,2,256]{3,2,1,0:T(2,128)}) %all-reduce.9.cloned.1.call-update) | async-done | bytes 524304 | tf_op jit(solution)/shard_map/psum | solution.py:76
  181.2 1.8 dynamic-slice_select_fusion
  183.0 35.2 %all-reduce.11.cloned.1.call-done = f32[16,16,2,128]{3,2,1,0:T(2,128)} async-done(((f32[16,16,2,128]{3,2,1,0:T(2,128)}), f32[16,16,2,128]{3,2,1,0:T(2,128)}) %all-reduce.11.cloned.1.call-update) | async-done | bytes 262160 | tf_op jit(solution)/shard_map/psum | solution.py:14
  218.2 1.8 multiply_add_fusion
  (30 shorter events, 5.9 us)
Async XLA Ops:
  6.5 2.7 %copy-start = (f32[16,16,2,128]{3,2,1,0:T(2,128)S(1)}, f32[16,16,2,128]{3,2,1,0:T(2,128)}, u32[]{:S(2)}) copy-start(f32[16,16,2,128]{3,2,1,0:T(2,128)} %param.3) | copy-start | bytes 786436
  6.5 71.1 %all-reduce.5.cloned.1.call-start = ((), (), s32[]{:S(2)}) async-start(), calls=%async_computation | async-start | bytes 1048576 | tf_op jit(solution)/shard_map/psum | solution.py:76
  20.2 94.5 %all-reduce.7.cloned.1.call-start = ((), (), s32[]{:S(2)}) async-start(), calls=%async_computation.1 | async-start | bytes 524288 | tf_op jit(solution)/shard_map/psum | solution.py:14
  79.4 101.8 %all-reduce.9.cloned.1.call-start = ((), (), s32[]{:S(2)}) async-start(), calls=%async_computation.2 | async-start | bytes 1048576 | tf_op jit(solution)/shard_map/psum | solution.py:76
  126.8 91.4 %all-reduce.11.cloned.1.call-start = ((), (), s32[]{:S(2)}) async-start(), calls=%async_computation.3 | async-start | bytes 524288 | tf_op jit(solution)/shard_map/psum | solution.py:14
Sparse Core Ops, SparseCore 0:
  20.3 57.2 all-reduce.4
  80.0 34.6 all-reduce.6
  126.9 54.2 all-reduce.8
  183.5 34.6 all-reduce.10
where the time goes:
time: 227 us
  waiting for transfers between devices  182 us (80%)
  local copies, waits for them, and re-layouts  14.9 us (7%)
  between operations  13.4 us (6%)
  other arithmetic  10.1 us (4%)
  matrix products  5.8 us (3%)
    psum x2, waiting for transfers between devices, per_device(): totals = lax.psum(partial_value, 'row')  112 us
    psum x2, waiting for transfers between devices, broadcast(): return lax.psum(jnp.where(mine, x, jnp.zeros_like(x)), axis)  70.2 us
    reshape x3, local copies, waits for them, and re-layouts, cubic_sigma(): swapped = current.reshape(count, orbits, parts, length // orbits, orbits)  6.82 us
    dot_general x16, matrix products, product(): jnp.dot(left, right, precision=lax.Precision.HIGHEST, preferred_element_t...  5.8 us
  transfers between devices with their start and end apart: 4, of which 4 were waited for; matrix products, arithmetic and copies ran while one was open for 0% of the time, Pallas kernels for 0%

commit v1 on v0

v1 whole, which is shorter than its diff:
```python
import functools

import jax
import jax.numpy as jnp
from jax import lax
from jax.experimental import pallas as pl
from jax.experimental.pallas import tpu as pltpu
from jax.sharding import PartitionSpec as P

ITERS = 2
STEP_WEIGHT = 0.5
MOST_CHUNKS = 4
MESH = pl.DeviceIdType.MESH


def split(value):
    high = value.astype(jnp.bfloat16)
    low = (value - high.astype(jnp.float32)).astype(jnp.bfloat16)
    return high, low


def swap_orbits(real_part, imag_part, orbits):
    rows, lanes = real_part.shape
    blocks = lanes // orbits
    turned = jnp.concatenate([real_part, imag_part], axis=0).T
    pieces = [turned[at * orbits:(at + 1) * orbits] for at in range(blocks)]
    block_of_lane = lax.broadcasted_iota(jnp.int32, (orbits, lanes), 1) // orbits
    step = 1
    while step < blocks:
        low_side = (block_of_lane // step) % 2 == 0
        for at in range(blocks):
            if at & step:
                continue
            first, second = pieces[at], pieces[at + step]
            pieces[at] = jnp.where(low_side, first, pltpu.roll(second, step * orbits, 1))
            pieces[at + step] = jnp.where(low_side, pltpu.roll(first, lanes - step * orbits, 1), second)
        step *= 2
    whole = jnp.concatenate(pieces, axis=0)
    return whole[:rows], whole[rows:]


def cubic_sigma(real_part, imag_part, orbits):
    other_re, other_im = swap_orbits(real_part, imag_part, orbits)
    square_re = real_part * real_part - imag_part * imag_part
    square_im = 2.0 * real_part * imag_part
    return square_re * other_re + square_im * other_im, square_im * other_re - square_re * other_im


def kernel(
    n, chunks, orbits,
    front_ref, green_ref, field_ref, out_ref,
    b_high, b_low, pair_out, pair_in, own, rs_out, rs_in, total, z_in, done,
    pair_ss, pair_rs, rs_ss, rs_rs, z_ss, z_rs, done_ss, done_rs,
):
    row, plane = lax.axis_index("row"), lax.axis_index("col")
    chip, core = row // 2, row % 2
    rows, lanes = front_ref.shape[0] // 2, front_ref.shape[1]
    chunk_rows = rows // chunks
    unit = chunk_rows // n
    group = lanes // 2

    def at_chip(other):
        return (other * 2 + core, plane)

    def at_plane(other):
        return (row, other)

    sibling = (chip * 2 + 1 - core, plane)
    chips = [lax.rem(chip + d, n) for d in range(n)]
    planes = [lax.rem(plane + d, n) for d in range(n)]

    barrier = pltpu.get_barrier_semaphore()
    peers = [sibling] + [at_chip(chips[d]) for d in range(1, n)] + [at_plane(planes[d]) for d in range(1, n)]
    for peer in peers:
        pl.semaphore_signal(barrier, inc=1, device_id=peer, device_id_type=MESH)

    depth = green_ref.shape[0] // 4
    for half in range(2):
        at = 0
        for history in (green_ref, field_ref):
            real_part = history[pl.ds(2 * half, depth, stride=4), :]
            imag_part = history[pl.ds(2 * half + 1, depth, stride=4), :]
            real_high, real_low = split(real_part)
            imag_high, imag_low = split(imag_part)
            for store, re, im in ((b_high, real_high, imag_high), (b_low, real_low, imag_low)):
                store[half, at:at + depth, :lanes] = re
                store[half, at:at + depth, lanes:] = im
                store[half, at + depth:at + 2 * depth, :lanes] = -im
                store[half, at + depth:at + 2 * depth, lanes:] = re
            at += 2 * depth

    def remote(src, dst, send_sem, recv_sem, device):
        return pltpu.make_async_remote_copy(
            src_ref=src, dst_ref=dst, send_sem=send_sem, recv_sem=recv_sem, device_id=device, device_id_type=MESH
        )

    def pair_copy(it, h):
        return remote(pair_out.at[it, h], pair_in.at[it, h], pair_ss.at[it, h], pair_rs.at[it, h], sibling)

    def rs_copy(it, h, d):
        to = chips[d]
        return remote(rs_out.at[it, h, to], rs_in.at[it, h, d], rs_ss.at[it, h, d], rs_rs.at[it, h, d], at_chip(to))

    def z_copy(it, h, d):
        return remote(total.at[it, h], z_in.at[it, h, plane], z_ss.at[it, h, d], z_rs.at[it, h, plane], at_plane(planes[d]))

    def z_done_copy(it, h, d):
        return remote(total.at[it, h], done.at[it, h, chip], z_ss.at[it, h, d], done_rs.at[it, h, chip], at_plane(planes[d]))

    def done_copy(it, h, to, src):
        return remote(src, done.at[it, h, chip], done_ss.at[it, h, to], done_rs.at[it, h, chip], at_chip(to))

    def front(h, part):
        return front_ref[pl.ds(2 * h * chunk_rows + part, chunk_rows, stride=2), :]

    def arrived(it, h, part):
        return jnp.concatenate([done[it, h, p, part] for p in range(n)], axis=0)

    def current(it, h):
        if it == 0:
            return front(h, 0), front(h, 1)
        return tuple(front(h, part) + STEP_WEIGHT * arrived(it - 1, h, part) for part in range(2))

    def multiply(it, h):
        real_part, imag_part = current(it, h)
        sigmas = [
            cubic_sigma(real_part[at:at + group], imag_part[at:at + group], orbits)
            for at in range(0, chunk_rows, group)
        ]
        sigma_re = jnp.concatenate([s[0] for s in sigmas], axis=0)
        sigma_im = jnp.concatenate([s[1] for s in sigmas], axis=0)
        high, low = split(jnp.concatenate([sigma_re, sigma_im, real_part, imag_part], axis=1))
        both = jnp.concatenate([high, low], axis=0)
        for half, store in ((1 - core, pair_out.at[it]), (core, own)):
            upper = jnp.dot(both, b_high[half], preferred_element_type=jnp.float32)
            image = upper[:chunk_rows] + upper[chunk_rows:]
            image = image + jnp.dot(high, b_low[half], preferred_element_type=jnp.float32)
            store[h, 0] = image[:, :lanes]
            store[h, 1] = image[:, lanes:]
            if store is not own:
                if it == 0 and h == 0:
                    pl.semaphore_wait(barrier, len(peers))
                pair_copy(it, h).start()

    def add_pair(it, h):
        pair_copy(it, h).wait_recv()
        for d in list(range(1, n)) + [0]:
            to = chips[d]
            place = pl.ds(pl.multiple_of(to * unit, unit), unit)
            for part in range(2):
                rs_out[it, h, to, part] = own[h, part, place, :] + pair_in[it, h, part, place, :]
            if d:
                rs_copy(it, h, d).start()

    def add_chips(it, h):
        for d in range(1, n):
            rs_copy(it, h, d).wait_recv()
        value = rs_out[it, h, chip]
        for d in range(1, n):
            value = value + rs_in[it, h, d]
        total[it, h] = value

        @pl.when(chip == plane)
        def _():
            for d in range(1, n):
                z_done_copy(it, h, d).start()
            done[it, h, chip] = value

        @pl.when(chip != plane)
        def _():
            for d in range(1, n):
                z_copy(it, h, d).start()
            done_copy(it, h, plane, total.at[it, h]).start()

    def forward(it, h):
        for d in range(1, n):
            to = chips[d]

            @pl.when(to != plane)
            def _():
                landed = z_in.at[it, h, to]
                remote(landed, landed, z_ss.at[it, h, d], z_rs.at[it, h, to], at_plane(to)).wait_recv()
                done_copy(it, h, to, landed).start()

    def settle(it, h):
        for d in range(1, n):
            source = chips[d]
            landed = done.at[it, h, source]
            remote(landed, landed, done_ss.at[it, h, source], done_rs.at[it, h, source], at_chip(source)).wait_recv()

        @pl.when(chip != plane)
        def _():
            landed = done.at[it, h, chip]
            remote(landed, landed, done_ss.at[it, h, chip], done_rs.at[it, h, chip], at_plane(chip)).wait_recv()

    def finish(it, h):
        settle(it, h)
        if it == ITERS - 1:
            for part in range(2):
                place = pl.ds(2 * h * chunk_rows + part, chunk_rows, stride=2)
                out_ref[place, :] = front(h, part) + STEP_WEIGHT * arrived(it, h, part)

    stages = (multiply, add_pair, add_chips, forward, finish)
    tasks = [
        (it * len(stages) + at + h, it, at, h)
        for it in range(ITERS) for at in range(len(stages)) for h in range(chunks)
    ]
    for _, it, at, h in sorted(tasks, key=lambda task: (task[0], task[3])):
        stages[at](it, h)

    for it in range(ITERS):
        for h in range(chunks):
            pair_copy(it, h).wait_send()
            for d in range(1, n):
                rs_copy(it, h, d).wait_send()
                z_copy(it, h, d).wait_send()
                done_copy(it, h, chips[d], total.at[it, h]).wait_send()


def per_device(front_init, green_hist, field_hist):
    n = lax.axis_size("col")
    if lax.axis_size("row") != 2 * n or green_hist.shape[3] != 2 * front_init.shape[3]:
        raise ValueError("unexpected mesh")
    count, orbits, parts, lanes = front_init.shape
    rows = count * orbits
    chunks = max(1, min(MOST_CHUNKS, rows // (8 * n), 2 * rows // lanes))
    unit = rows // (chunks * n)

    def flat(history):
        steps, depth = history.shape[:2]
        return history.reshape(steps * depth, parts, 2, lanes).transpose(0, 2, 1, 3).reshape(-1, lanes)

    def vmem(*shape):
        return pltpu.VMEM(shape, jnp.float32)

    depth = green_hist.shape[0] * green_hist.shape[1]
    lead = (ITERS, chunks)
    sems = lambda *shape: pltpu.SemaphoreType.DMA(shape)
    result = pl.pallas_call(
        functools.partial(kernel, n, chunks, orbits),
        out_shape=jax.ShapeDtypeStruct((rows * parts, lanes), jnp.float32),
        in_specs=[pl.BlockSpec(memory_space=pltpu.VMEM)] * 3,
        out_specs=pl.BlockSpec(memory_space=pltpu.VMEM),
        scratch_shapes=[
            pltpu.VMEM((2, 4 * depth, 2 * lanes), jnp.bfloat16),
            pltpu.VMEM((2, 4 * depth, 2 * lanes), jnp.bfloat16),
            vmem(*lead, 2, rows // chunks, lanes),
            vmem(*lead, 2, rows // chunks, lanes),
            vmem(chunks, 2, rows // chunks, lanes),
            vmem(*lead, n, 2, unit, lanes),
            vmem(*lead, n, 2, unit, lanes),
            vmem(*lead, 2, unit, lanes),
            vmem(*lead, n, 2, unit, lanes),
            vmem(*lead, n, 2, unit, lanes),
            sems(*lead), sems(*lead),
            sems(*lead, n), sems(*lead, n),
            sems(*lead, n), sems(*lead, n),
            sems(*lead, n), sems(*lead, n),
        ],
        compiler_params=pltpu.CompilerParams(
            collective_id=0, has_side_effects=True, vmem_limit_bytes=40 * 1024 * 1024
        ),
    )(front_init.reshape(rows * parts, lanes), flat(green_hist), flat(field_hist))
    return result.reshape(front_init.shape)


def solution(mesh):
    in_specs = (
        P(None, None, None, "row"),
        P("row", None, None, "col"),
        P("row", None, None, "col"),
    )
    out_specs = P(None, None, None, "row")
    return jax.shard_map(
        per_device, mesh=mesh, in_specs=in_specs, out_specs=out_specs, check_vma=False
    )
```

time: 227 us -> 47.8 us (0.21)
  the two profiles are of different devices: /device:TPU:0 before, /device:TPU:2 now
where the time goes in v1:
time: 47.8 us; the launch traced here: 47.6 us
  Pallas kernels  44 us (92%)
  local copies, waits for them, and re-layouts  3.55 us (7%)
    pallas_call x1, Pallas kernels, per_device(): pl.pallas_call(functools.partial(kernel, n, chunks, orbits), out_shape=ja...  44 us
    unnamed x7, local copies, waits for them, and re-layouts  3.55 us

profile of v1, /device:TPU:2, one launch (start us, length us, event | category | flops | bytes accessed | tf_op | source)
XLA Modules:
  0.0 47.6 jit_solution(16672087837952202878)
XLA Ops:
  0.0 0.0 copy-start
  0.0 0.9 %copy-done = f32[16,16,2,128]{3,2,1,0:T(2,128)S(1)} copy-done((f32[16,16,2,128]{3,2,1,0:T(2,128)S(1)}, f32[16,16,2,128]{3,2,1,0:T(2,128)}, u32[]{:S(2)}) %copy-start) | copy-done | bytes 262168
  1.0 0.0 copy-start.1
  1.0 0.9 %copy-done.1 = f32[8,16,2,256]{3,2,1,0:T(2,128)S(1)} copy-done((f32[8,16,2,256]{3,2,1,0:T(2,128)S(1)}, f32[8,16,2,256]{3,2,1,0:T(2,128)}, u32[]{:S(2)}) %copy-start.1) | copy-done | bytes 262168
  1.9 0.0 copy-start.2
  1.9 0.9 %copy-done.2 = f32[8,16,2,256]{3,2,1,0:T(2,128)S(1)} copy-done((f32[8,16,2,256]{3,2,1,0:T(2,128)S(1)}, f32[8,16,2,256]{3,2,1,0:T(2,128)}, u32[]{:S(2)}) %copy-start.2) | copy-done | bytes 262168
  2.9 44.0 %shard_map.37 = f32[512,128]{1,0:T(8,128)S(1)} custom-call(f32[512,128]{1,0:T(8,128)S(1)} %bitcast.13, f32[512,128]{1,0:T(8,128)S(1)} %bitcast.14, f32[512,128]{1,0:T(8,128)S(1)} %bitcast.15), custom_call_target="tpu_custom_call" | custom-call | tf_op jit(solution)/shard_map/pallas_call | solution.py:239
  46.9 0.7 %copy.7 = f32[16,16,2,128]{3,2,1,0:T(2,128)} copy(f32[16,16,2,128]{3,2,1,0:T(2,128)S(1)} %bitcast.12) | data formatting | bytes 524288
Async XLA Ops:
  0.0 0.9 %copy-start = (f32[16,16,2,128]{3,2,1,0:T(2,128)S(1)}, f32[16,16,2,128]{3,2,1,0:T(2,128)}, u32[]{:S(2)}) copy-start(f32[16,16,2,128]{3,2,1,0:T(2,128)} %param.3) | copy-start | bytes 786436
  1.0 0.9 %copy-start.1 = (f32[8,16,2,256]{3,2,1,0:T(2,128)S(1)}, f32[8,16,2,256]{3,2,1,0:T(2,128)}, u32[]{:S(2)}) copy-start(f32[8,16,2,256]{3,2,1,0:T(2,128)} %param.4) | copy-start | bytes 786436
  1.9 0.9 %copy-start.2 = (f32[8,16,2,256]{3,2,1,0:T(2,128)S(1)}, f32[8,16,2,256]{3,2,1,0:T(2,128)}, u32[]{:S(2)}) copy-start(f32[8,16,2,256]{3,2,1,0:T(2,128)} %param.5) | copy-start | bytes 786436

commit v2 on v1

--- a/solution.py
+++ b/solution.py
@@ -9,7 +9,7 @@
 
 ITERS = 2
 STEP_WEIGHT = 0.5
-MOST_CHUNKS = 4
+MOST_CHUNKS = 2
 MESH = pl.DeviceIdType.MESH
 
 
@@ -48,8 +48,8 @@
 
 def kernel(
     n, chunks, orbits,
-    front_ref, green_ref, field_ref, out_ref,
-    b_high, b_low, pair_out, pair_in, own, rs_out, rs_in, total, z_in, done,
+    front_hbm, green_hbm, field_hbm, out_ref,
+    front_ref, green_ref, field_ref, load_sem, b_high, b_low, pair_out, pair_in, own, rs_out, rs_in, total, z_in, done,
     pair_ss, pair_rs, rs_ss, rs_rs, z_ss, z_rs, done_ss, done_rs,
 ):
     row, plane = lax.axis_index("row"), lax.axis_index("col")
@@ -69,11 +69,20 @@
     chips = [lax.rem(chip + d, n) for d in range(n)]
     planes = [lax.rem(plane + d, n) for d in range(n)]
 
+    loads = [
+        pltpu.make_async_copy(src, dst, load_sem.at[at])
+        for at, (src, dst) in enumerate(((green_hbm, green_ref), (field_hbm, field_ref), (front_hbm, front_ref)))
+    ]
+    for load in loads:
+        load.start()
+
     barrier = pltpu.get_barrier_semaphore()
     peers = [sibling] + [at_chip(chips[d]) for d in range(1, n)] + [at_plane(planes[d]) for d in range(1, n)]
     for peer in peers:
         pl.semaphore_signal(barrier, inc=1, device_id=peer, device_id_type=MESH)
 
+    for load in loads:
+        load.wait()
     depth = green_ref.shape[0] // 4
     for half in range(2):
         at = 0
@@ -239,9 +248,13 @@
     result = pl.pallas_call(
         functools.partial(kernel, n, chunks, orbits),
         out_shape=jax.ShapeDtypeStruct((rows * parts, lanes), jnp.float32),
-        in_specs=[pl.BlockSpec(memory_space=pltpu.VMEM)] * 3,
+        in_specs=[pl.BlockSpec(memory_space=pl.ANY)] * 3,
         out_specs=pl.BlockSpec(memory_space=pltpu.VMEM),
         scratch_shapes=[
+            vmem(rows * parts, lanes),
+            vmem(4 * depth, lanes),
+            vmem(4 * depth, lanes),
+            sems(3),
             pltpu.VMEM((2, 4 * depth, 2 * lanes), jnp.bfloat16),
             pltpu.VMEM((2, 4 * depth, 2 * lanes), jnp.bfloat16),
             vmem(*lead, 2, rows // chunks, lanes),
@@ -258,7 +271,7 @@
             sems(*lead, n), sems(*lead, n),
         ],
         compiler_params=pltpu.CompilerParams(
-            collective_id=0, has_side_effects=True, vmem_limit_bytes=40 * 1024 * 1024
+            collective_id=0, has_side_effects=True, vmem_limit_bytes=56 * 1024 * 1024
         ),
     )(front_init.reshape(rows * parts, lanes), flat(green_hist), flat(field_hist))
     return result.reshape(front_init.shape)

time: 47.8 us -> 40.5 us (0.85)
  Pallas kernels: 44 us -> 38.6 us
  local copies, waits for them, and re-layouts: 3.55 us -> 1.67 us
    pallas_call x1, Pallas kernels: 44 us -> 38.6 us  [per_device(): pl.pallas_call(functools.partial(kernel, n, chunks, orbits), out_shape=ja...]
    unnamed x7 -> x1, local copies, waits for them, and re-layouts: 3.55 us -> 1.67 us
where the time goes in v2:
time: 40.5 us; the launch traced here: 40.3 us
  Pallas kernels  38.6 us (95%)
  local copies, waits for them, and re-layouts  1.67 us (4%)
    pallas_call x1, Pallas kernels, per_device(): pl.pallas_call(functools.partial(kernel, n, chunks, orbits), out_shape=ja...  38.6 us
    unnamed x1, local copies, waits for them, and re-layouts  1.67 us

profile of v2, /device:TPU:2, one launch (start us, length us, event | category | flops | bytes accessed | tf_op | source)
XLA Modules:
  0.0 40.3 jit_solution(8934375202705362051)
XLA Ops:
  0.0 38.6 %shard_map.37 = f32[512,128]{1,0:T(8,128)} custom-call(f32[512,128]{1,0:T(8,128)} %bitcast.13, f32[512,128]{1,0:T(8,128)} %bitcast.14, f32[512,128]{1,0:T(8,128)} %bitcast.15), custom_call_target="tpu_custom_call" | custom-call | tf_op jit(solution)/shard_map/pallas_call | solution.py:248
  38.6 1.7 %copy.7 = f32[16,16,2,128]{3,2,1,0:T(2,128)} copy(f32[16,16,2,128]{3,2,1,0:T(2,128)} %bitcast.12) | data formatting | bytes 524288

commit v3 on v2

--- a/solution.py
+++ b/solution.py
@@ -49,8 +49,8 @@
 def kernel(
     n, chunks, orbits,
     front_hbm, green_hbm, field_hbm, out_ref,
-    front_ref, green_ref, field_ref, load_sem, b_high, b_low, pair_out, pair_in, own, rs_out, rs_in, total, z_in, done,
-    pair_ss, pair_rs, rs_ss, rs_rs, z_ss, z_rs, done_ss, done_rs,
+    front_ref, green_ref, field_ref, load_sem, b_high, b_low, pair_out, pair_in, own, rs_out, rs_in, total, done,
+    pair_ss, pair_rs, rs_ss, rs_rs, done_ss, done_rs,
 ):
     row, plane = lax.axis_index("row"), lax.axis_index("col")
     chip, core = row // 2, row % 2
@@ -62,9 +62,6 @@
     def at_chip(other):
         return (other * 2 + core, plane)
 
-    def at_plane(other):
-        return (row, other)
-
     sibling = (chip * 2 + 1 - core, plane)
     chips = [lax.rem(chip + d, n) for d in range(n)]
     planes = [lax.rem(plane + d, n) for d in range(n)]
@@ -77,9 +74,13 @@
         load.start()
 
     barrier = pltpu.get_barrier_semaphore()
-    peers = [sibling] + [at_chip(chips[d]) for d in range(1, n)] + [at_plane(planes[d]) for d in range(1, n)]
-    for peer in peers:
-        pl.semaphore_signal(barrier, inc=1, device_id=peer, device_id_type=MESH)
+    for source in [sibling] + [at_chip(chips[d]) for d in range(1, n)]:
+        pl.semaphore_signal(barrier, inc=1, device_id=source, device_id_type=MESH)
+
+    @pl.when(chip != plane)
+    def _():
+        for d in range(n):
+            pl.semaphore_signal(barrier, inc=1, device_id=(chips[d] * 2 + core, chip), device_id_type=MESH)
 
     for load in loads:
         load.wait()
@@ -110,14 +111,9 @@
         to = chips[d]
         return remote(rs_out.at[it, h, to], rs_in.at[it, h, d], rs_ss.at[it, h, d], rs_rs.at[it, h, d], at_chip(to))
 
-    def z_copy(it, h, d):
-        return remote(total.at[it, h], z_in.at[it, h, plane], z_ss.at[it, h, d], z_rs.at[it, h, plane], at_plane(planes[d]))
-
-    def z_done_copy(it, h, d):
-        return remote(total.at[it, h], done.at[it, h, chip], z_ss.at[it, h, d], done_rs.at[it, h, chip], at_plane(planes[d]))
-
-    def done_copy(it, h, to, src):
-        return remote(src, done.at[it, h, chip], done_ss.at[it, h, to], done_rs.at[it, h, chip], at_chip(to))
+    def done_copy(it, h, d):
+        to = (plane * 2 + core, planes[d])
+        return remote(total.at[it, h], done.at[it, h, chip], done_ss.at[it, h, d], done_rs.at[it, h, chip], to)
 
     def front(h, part):
         return front_ref[pl.ds(2 * h * chunk_rows + part, chunk_rows, stride=2), :]
@@ -148,7 +144,7 @@
             store[h, 1] = image[:, lanes:]
             if store is not own:
                 if it == 0 and h == 0:
-                    pl.semaphore_wait(barrier, len(peers))
+                    pl.semaphore_wait(barrier, 2 * n - 1)
                 pair_copy(it, h).start()
 
     def add_pair(it, h):
@@ -169,27 +165,16 @@
             value = value + rs_in[it, h, d]
         total[it, h] = value
 
+        for d in range(1, n):
+            done_copy(it, h, d).start()
+
+        @pl.when(chip != plane)
+        def _():
+            done_copy(it, h, 0).start()
+
         @pl.when(chip == plane)
         def _():
-            for d in range(1, n):
-                z_done_copy(it, h, d).start()
             done[it, h, chip] = value
-
-        @pl.when(chip != plane)
-        def _():
-            for d in range(1, n):
-                z_copy(it, h, d).start()
-            done_copy(it, h, plane, total.at[it, h]).start()
-
-    def forward(it, h):
-        for d in range(1, n):
-            to = chips[d]
-
-            @pl.when(to != plane)
-            def _():
-                landed = z_in.at[it, h, to]
-                remote(landed, landed, z_ss.at[it, h, d], z_rs.at[it, h, to], at_plane(to)).wait_recv()
-                done_copy(it, h, to, landed).start()
 
     def settle(it, h):
         for d in range(1, n):
@@ -200,7 +185,7 @@
         @pl.when(chip != plane)
         def _():
             landed = done.at[it, h, chip]
-            remote(landed, landed, done_ss.at[it, h, chip], done_rs.at[it, h, chip], at_plane(chip)).wait_recv()
+            remote(landed, landed, done_ss.at[it, h, chip], done_rs.at[it, h, chip], (row, chip)).wait_recv()
 
     def finish(it, h):
         settle(it, h)
@@ -209,7 +194,7 @@
                 place = pl.ds(2 * h * chunk_rows + part, chunk_rows, stride=2)
                 out_ref[place, :] = front(h, part) + STEP_WEIGHT * arrived(it, h, part)
 
-    stages = (multiply, add_pair, add_chips, forward, finish)
+    stages = (multiply, add_pair, add_chips, finish)
     tasks = [
         (it * len(stages) + at + h, it, at, h)
         for it in range(ITERS) for at in range(len(stages)) for h in range(chunks)
@@ -222,8 +207,11 @@
             pair_copy(it, h).wait_send()
             for d in range(1, n):
                 rs_copy(it, h, d).wait_send()
-                z_copy(it, h, d).wait_send()
-                done_copy(it, h, chips[d], total.at[it, h]).wait_send()
+                done_copy(it, h, d).wait_send()
+
+            @pl.when(chip != plane)
+            def _():
+                done_copy(it, h, 0).wait_send()
 
 
 def per_device(front_init, green_hist, field_hist):
@@ -264,9 +252,7 @@
             vmem(*lead, n, 2, unit, lanes),
             vmem(*lead, 2, unit, lanes),
             vmem(*lead, n, 2, unit, lanes),
-            vmem(*lead, n, 2, unit, lanes),
             sems(*lead), sems(*lead),
-            sems(*lead, n), sems(*lead, n),
             sems(*lead, n), sems(*lead, n),
             sems(*lead, n), sems(*lead, n),
         ],

time: 40.5 us -> 36.6 us (0.904)
  the two profiles are of different devices: /device:TPU:2 before, /device:TPU:0 now
where the time goes in v3:
time: 36.6 us; the launch traced here: 36.4 us
  Pallas kernels  34.7 us (95%)
  local copies, waits for them, and re-layouts  1.67 us (5%)
    pallas_call x1, Pallas kernels, per_device(): pl.pallas_call(functools.partial(kernel, n, chunks, orbits), out_shape=ja...  34.7 us
    unnamed x1, local copies, waits for them, and re-layouts  1.67 us

profile of v3, /device:TPU:0, one launch (start us, length us, event | category | flops | bytes accessed | tf_op | source)
XLA Modules:
  0.0 36.4 jit_solution(16159286274716418954)
XLA Ops:
  0.0 34.7 %shard_map.37 = f32[512,128]{1,0:T(8,128)} custom-call(f32[512,128]{1,0:T(8,128)} %bitcast.13, f32[512,128]{1,0:T(8,128)} %bitcast.14, f32[512,128]{1,0:T(8,128)} %bitcast.15), custom_call_target="tpu_custom_call" | custom-call | tf_op jit(solution)/shard_map/pallas_call | solution.py:236
  34.7 1.7 %copy.7 = f32[16,16,2,128]{3,2,1,0:T(2,128)} copy(f32[16,16,2,128]{3,2,1,0:T(2,128)} %bitcast.12) | data formatting | bytes 524288

commit v4 on v3

--- a/solution.py
+++ b/solution.py
@@ -189,6 +189,8 @@
 
     def finish(it, h):
         settle(it, h)
+        if it < ITERS - 1:
+            multiply(it + 1, h)
         if it == ITERS - 1:
             for part in range(2):
                 place = pl.ds(2 * h * chunk_rows + part, chunk_rows, stride=2)
@@ -196,10 +198,11 @@
 
     stages = (multiply, add_pair, add_chips, finish)
     tasks = [
-        (it * len(stages) + at + h, it, at, h)
+        (it, at, h)
         for it in range(ITERS) for at in range(len(stages)) for h in range(chunks)
+        if it == 0 or at > 0
     ]
-    for _, it, at, h in sorted(tasks, key=lambda task: (task[0], task[3])):
+    for it, at, h in tasks:
         stages[at](it, h)
 
     for it in range(ITERS):
@@ -236,7 +239,7 @@
     result = pl.pallas_call(
         functools.partial(kernel, n, chunks, orbits),
         out_shape=jax.ShapeDtypeStruct((rows * parts, lanes), jnp.float32),
-        in_specs=[pl.BlockSpec(memory_space=pl.ANY)] * 3,
+        in_specs=[pl.BlockSpec(memory_space=pltpu.HBM)] * 3,
         out_specs=pl.BlockSpec(memory_space=pltpu.VMEM),
         scratch_shapes=[
             vmem(rows * parts, lanes),
@@ -257,7 +260,7 @@
             sems(*lead, n), sems(*lead, n),
         ],
         compiler_params=pltpu.CompilerParams(
-            collective_id=0, has_side_effects=True, vmem_limit_bytes=56 * 1024 * 1024
+            collective_id=0, has_side_effects=True, vmem_limit_bytes=16 * 1024 * 1024
         ),
     )(front_init.reshape(rows * parts, lanes), flat(green_hist), flat(field_hist))
     return result.reshape(front_init.shape)

time: 36.6 us -> 34.5 us (0.943)
  the two profiles are of different devices: /device:TPU:0 before, /device:TPU:6 now
where the time goes in v4:
time: 34.5 us; the launch traced here: 34.3 us
  Pallas kernels  30.7 us (89%)
  local copies, waits for them, and re-layouts  3.55 us (10%)
    pallas_call x1, Pallas kernels, per_device(): pl.pallas_call(functools.partial(kernel, n, chunks, orbits), out_shape=ja...  30.7 us
    unnamed x7, local copies, waits for them, and re-layouts  3.55 us

profile of v4, /device:TPU:6, one launch (start us, length us, event | category | flops | bytes accessed | tf_op | source)
XLA Modules:
  0.0 34.3 jit_solution(3635818471180314228)
XLA Ops:
  0.0 0.0 copy-start
  0.0 0.9 %copy-done = f32[16,16,2,128]{3,2,1,0:T(2,128)S(1)} copy-done((f32[16,16,2,128]{3,2,1,0:T(2,128)S(1)}, f32[16,16,2,128]{3,2,1,0:T(2,128)}, u32[]{:S(2)}) %copy-start) | copy-done | bytes 262168
  1.0 0.0 copy-start.1
  1.0 0.9 %copy-done.1 = f32[8,16,2,256]{3,2,1,0:T(2,128)S(1)} copy-done((f32[8,16,2,256]{3,2,1,0:T(2,128)S(1)}, f32[8,16,2,256]{3,2,1,0:T(2,128)}, u32[]{:S(2)}) %copy-start.1) | copy-done | bytes 262168
  1.9 0.0 copy-start.2
  1.9 0.9 %copy-done.2 = f32[8,16,2,256]{3,2,1,0:T(2,128)S(1)} copy-done((f32[8,16,2,256]{3,2,1,0:T(2,128)S(1)}, f32[8,16,2,256]{3,2,1,0:T(2,128)}, u32[]{:S(2)}) %copy-start.2) | copy-done | bytes 262168
  2.9 30.7 %shard_map.37 = f32[512,128]{1,0:T(8,128)S(1)} custom-call(f32[512,128]{1,0:T(8,128)S(1)} %bitcast.13, f32[512,128]{1,0:T(8,128)S(1)} %bitcast.14, f32[512,128]{1,0:T(8,128)S(1)} %bitcast.15), custom_call_target="tpu_custom_call" | custom-call | tf_op jit(solution)/shard_map/pallas_call | solution.py:239
  33.6 0.7 %copy.7 = f32[16,16,2,128]{3,2,1,0:T(2,128)} copy(f32[16,16,2,128]{3,2,1,0:T(2,128)S(1)} %bitcast.12) | data formatting | bytes 524288
Async XLA Ops:
  0.0 0.9 %copy-start = (f32[16,16,2,128]{3,2,1,0:T(2,128)S(1)}, f32[16,16,2,128]{3,2,1,0:T(2,128)}, u32[]{:S(2)}) copy-start(f32[16,16,2,128]{3,2,1,0:T(2,128)} %param.3) | copy-start | bytes 786436
  1.0 0.9 %copy-start.1 = (f32[8,16,2,256]{3,2,1,0:T(2,128)S(1)}, f32[8,16,2,256]{3,2,1,0:T(2,128)}, u32[]{:S(2)}) copy-start(f32[8,16,2,256]{3,2,1,0:T(2,128)} %param.4) | copy-start | bytes 786436
  1.9 0.9 %copy-start.2 = (f32[8,16,2,256]{3,2,1,0:T(2,128)S(1)}, f32[8,16,2,256]{3,2,1,0:T(2,128)}, u32[]{:S(2)}) copy-start(f32[8,16,2,256]{3,2,1,0:T(2,128)} %param.5) | copy-start | bytes 786436

commit v5 on v4

--- a/solution.py
+++ b/solution.py
@@ -9,7 +9,8 @@
 
 ITERS = 2
 STEP_WEIGHT = 0.5
-MOST_CHUNKS = 2
+MOST_CHUNKS = 4
+VMEM_LIMIT = 54784 * 1024
 MESH = pl.DeviceIdType.MESH
 
 
@@ -46,6 +47,13 @@
     return square_re * other_re + square_im * other_im, square_im * other_re - square_re * other_im
 
 
+def expected(chunks, it, at, h):
+    if at == 3:
+        return 8.3 * (it + 1) + 5.2 / chunks * h
+    start = 8.3 * it + (5.2 if it else 2.8) / chunks * h
+    return start + (0.0, 1.65, 3.85)[at]
+
+
 def kernel(
     n, chunks, orbits,
     front_hbm, green_hbm, field_hbm, out_ref,
@@ -85,18 +93,21 @@
     for load in loads:
         load.wait()
     depth = green_ref.shape[0] // 4
-    for half in range(2):
+
+    def prepare(side):
         at = 0
         for history in (green_ref, field_ref):
-            real_part = history[pl.ds(2 * half, depth, stride=4), :]
-            imag_part = history[pl.ds(2 * half + 1, depth, stride=4), :]
-            real_high, real_low = split(real_part)
-            imag_high, imag_low = split(imag_part)
+            parts = []
+            for part in range(2):
+                halves = [history[pl.ds(2 * half + part, depth, stride=4), :] for half in range(2)]
+                parts.append(jnp.where(core == side, halves[1], halves[0]))
+            real_high, real_low = split(parts[0])
+            imag_high, imag_low = split(parts[1])
             for store, re, im in ((b_high, real_high, imag_high), (b_low, real_low, imag_low)):
-                store[half, at:at + depth, :lanes] = re
-                store[half, at:at + depth, lanes:] = im
-                store[half, at + depth:at + 2 * depth, :lanes] = -im
-                store[half, at + depth:at + 2 * depth, lanes:] = re
+                store[side, at:at + depth, :lanes] = re
+                store[side, at:at + depth, lanes:] = im
+                store[side, at + depth:at + 2 * depth, :lanes] = -im
+                store[side, at + depth:at + 2 * depth, lanes:] = re
             at += 2 * depth
 
     def remote(src, dst, send_sem, recv_sem, device):
@@ -136,10 +147,12 @@
         sigma_im = jnp.concatenate([s[1] for s in sigmas], axis=0)
         high, low = split(jnp.concatenate([sigma_re, sigma_im, real_part, imag_part], axis=1))
         both = jnp.concatenate([high, low], axis=0)
-        for half, store in ((1 - core, pair_out.at[it]), (core, own)):
-            upper = jnp.dot(both, b_high[half], preferred_element_type=jnp.float32)
+        for side, store in enumerate((pair_out.at[it], own)):
+            if it == 0 and h == 0:
+                prepare(side)
+            upper = jnp.dot(both, b_high[side], preferred_element_type=jnp.float32)
             image = upper[:chunk_rows] + upper[chunk_rows:]
-            image = image + jnp.dot(high, b_low[half], preferred_element_type=jnp.float32)
+            image = image + jnp.dot(high, b_low[side], preferred_element_type=jnp.float32)
             store[h, 0] = image[:, :lanes]
             store[h, 1] = image[:, lanes:]
             if store is not own:
@@ -202,6 +215,7 @@
         for it in range(ITERS) for at in range(len(stages)) for h in range(chunks)
         if it == 0 or at > 0
     ]
+    tasks.sort(key=lambda task: expected(chunks, *task))
     for it, at, h in tasks:
         stages[at](it, h)
 
@@ -260,7 +274,7 @@
             sems(*lead, n), sems(*lead, n),
         ],
         compiler_params=pltpu.CompilerParams(
-            collective_id=0, has_side_effects=True, vmem_limit_bytes=16 * 1024 * 1024
+            collective_id=0, has_side_effects=True, vmem_limit_bytes=VMEM_LIMIT
         ),
     )(front_init.reshape(rows * parts, lanes), flat(green_hist), flat(field_hist))
     return result.reshape(front_init.shape)

time: 34.5 us -> 31.5 us (0.913)
  the two profiles are of different devices: /device:TPU:6 before, /device:TPU:0 now
where the time goes in v5:
time: 31.5 us; the launch traced here: 31.3 us
  Pallas kernels  30.6 us (97%)
  local copies, waits for them, and re-layouts  0.71 us (2%)
    pallas_call x1, Pallas kernels, per_device(): pl.pallas_call(functools.partial(kernel, n, chunks, orbits), out_shape=ja...  30.6 us
    unnamed x1, local copies, waits for them, and re-layouts  0.71 us

profile of v5, /device:TPU:0, one launch (start us, length us, event | category | flops | bytes accessed | tf_op | source)
XLA Modules:
  0.0 31.3 jit_solution(11222891989523498818)
XLA Ops:
  0.0 30.6 %shard_map.37 = f32[512,128]{1,0:T(8,128)S(1)} custom-call(f32[512,128]{1,0:T(8,128)} %bitcast.13, f32[512,128]{1,0:T(8,128)} %bitcast.14, f32[512,128]{1,0:T(8,128)} %bitcast.15), custom_call_target="tpu_custom_call" | custom-call | tf_op jit(solution)/shard_map/pallas_call | solution.py:253
  30.6 0.7 %copy.7 = f32[16,16,2,128]{3,2,1,0:T(2,128)} copy(f32[16,16,2,128]{3,2,1,0:T(2,128)S(1)} %bitcast.12) | data formatting | bytes 524288

commit v6 on v5

--- a/solution.py
+++ b/solution.py
@@ -119,12 +119,30 @@
         return remote(pair_out.at[it, h], pair_in.at[it, h], pair_ss.at[it, h], pair_rs.at[it, h], sibling)
 
     def rs_copy(it, h, d):
-        to = chips[d]
-        return remote(rs_out.at[it, h, to], rs_in.at[it, h, d], rs_ss.at[it, h, d], rs_rs.at[it, h, d], at_chip(to))
+        return remote(rs_out.at[it, h, d], rs_in.at[it, h, d], rs_ss.at[it, h], rs_rs.at[it, h], at_chip(chips[d]))
+
+    def rs_all(it, h):
+        most = pl.ds(1, n - 1)
+        return remote(rs_out.at[it, h, most], rs_in.at[it, h, most], rs_ss.at[it, h], rs_rs.at[it, h], at_chip(chips[1]))
 
     def done_copy(it, h, d):
         to = (plane * 2 + core, planes[d])
-        return remote(total.at[it, h], done.at[it, h, chip], done_ss.at[it, h, d], done_rs.at[it, h, chip], to)
+        return remote(total.at[it, h], done.at[it, h, chip], done_ss.at[it, h], done_rs.at[it, h], to)
+
+    def done_all(it, h, count):
+        pieces = done.at[it, h, pl.ds(0, count)]
+        return remote(pieces, pieces, done_ss.at[it, h], done_rs.at[it, h], sibling)
+
+    def wait_done(it, h, send):
+        @pl.when(chip != plane)
+        def _():
+            copy = done_all(it, h, n)
+            copy.wait_send() if send else copy.wait_recv()
+
+        @pl.when(chip == plane)
+        def _():
+            copy = done_all(it, h, n - 1)
+            copy.wait_send() if send else copy.wait_recv()
 
     def front(h, part):
         return front_ref[pl.ds(2 * h * chunk_rows + part, chunk_rows, stride=2), :]
@@ -166,14 +184,13 @@
             to = chips[d]
             place = pl.ds(pl.multiple_of(to * unit, unit), unit)
             for part in range(2):
-                rs_out[it, h, to, part] = own[h, part, place, :] + pair_in[it, h, part, place, :]
+                rs_out[it, h, d, part] = own[h, part, place, :] + pair_in[it, h, part, place, :]
             if d:
                 rs_copy(it, h, d).start()
 
     def add_chips(it, h):
-        for d in range(1, n):
-            rs_copy(it, h, d).wait_recv()
-        value = rs_out[it, h, chip]
+        rs_all(it, h).wait_recv()
+        value = rs_out[it, h, 0]
         for d in range(1, n):
             value = value + rs_in[it, h, d]
         total[it, h] = value
@@ -189,19 +206,18 @@
         def _():
             done[it, h, chip] = value
 
-    def settle(it, h):
-        for d in range(1, n):
-            source = chips[d]
-            landed = done.at[it, h, source]
-            remote(landed, landed, done_ss.at[it, h, source], done_rs.at[it, h, source], at_chip(source)).wait_recv()
-
-        @pl.when(chip != plane)
-        def _():
-            landed = done.at[it, h, chip]
-            remote(landed, landed, done_ss.at[it, h, chip], done_rs.at[it, h, chip], (row, chip)).wait_recv()
+    def drain():
+        for it in range(ITERS):
+            for h in range(chunks):
+                pair_copy(it, h).wait_send()
+                rs_all(it, h).wait_send()
+                if it < ITERS - 1:
+                    wait_done(it, h, True)
 
     def finish(it, h):
-        settle(it, h)
+        if it == ITERS - 1 and h == 0:
+            drain()
+        wait_done(it, h, False)
         if it < ITERS - 1:
             multiply(it + 1, h)
         if it == ITERS - 1:
@@ -219,16 +235,8 @@
     for it, at, h in tasks:
         stages[at](it, h)
 
-    for it in range(ITERS):
-        for h in range(chunks):
-            pair_copy(it, h).wait_send()
-            for d in range(1, n):
-                rs_copy(it, h, d).wait_send()
-                done_copy(it, h, d).wait_send()
-
-            @pl.when(chip != plane)
-            def _():
-                done_copy(it, h, 0).wait_send()
+    for h in range(chunks):
+        wait_done(ITERS - 1, h, True)
 
 
 def per_device(front_init, green_hist, field_hist):
@@ -270,8 +278,8 @@
             vmem(*lead, 2, unit, lanes),
             vmem(*lead, n, 2, unit, lanes),
             sems(*lead), sems(*lead),
-            sems(*lead, n), sems(*lead, n),
-            sems(*lead, n), sems(*lead, n),
+            sems(*lead), sems(*lead),
+            sems(*lead), sems(*lead),
         ],
         compiler_params=pltpu.CompilerParams(
             collective_id=0, has_side_effects=True, vmem_limit_bytes=VMEM_LIMIT

time: 31.5 us -> 30.6 us (0.971)
  Pallas kernels: 30.6 us -> 29.7 us
    pallas_call x1, Pallas kernels: 30.6 us -> 29.7 us  [per_device(): pl.pallas_call(functools.partial(kernel, n, chunks, orbits), out_shape=ja...]
where the time goes in v6:
time: 30.6 us; the launch traced here: 30.4 us
  Pallas kernels  29.7 us (97%)
  local copies, waits for them, and re-layouts  0.71 us (2%)
    pallas_call x1, Pallas kernels, per_device(): pl.pallas_call(functools.partial(kernel, n, chunks, orbits), out_shape=ja...  29.7 us
    unnamed x1, local copies, waits for them, and re-layouts  0.71 us

profile of v6, /device:TPU:0, one launch (start us, length us, event | category | flops | bytes accessed | tf_op | source)
XLA Modules:
  0.0 30.4 jit_solution(15610938262066826431)
XLA Ops:
  0.0 29.7 %shard_map.37 = f32[512,128]{1,0:T(8,128)S(1)} custom-call(f32[512,128]{1,0:T(8,128)} %bitcast.13, f32[512,128]{1,0:T(8,128)} %bitcast.14, f32[512,128]{1,0:T(8,128)} %bitcast.15), custom_call_target="tpu_custom_call" | custom-call | tf_op jit(solution)/shard_map/pallas_call | solution.py:261
  29.7 0.7 %copy.7 = f32[16,16,2,128]{3,2,1,0:T(2,128)} copy(f32[16,16,2,128]{3,2,1,0:T(2,128)S(1)} %bitcast.12) | data formatting | bytes 524288

commit v7 on v6

--- a/solution.py
+++ b/solution.py
@@ -51,7 +51,7 @@
     if at == 3:
         return 8.3 * (it + 1) + 5.2 / chunks * h
     start = 8.3 * it + (5.2 if it else 2.8) / chunks * h
-    return start + (0.0, 1.65, 3.85)[at]
+    return start + ((0.0, 1.65, 3.85) if it else (0.0, 1.3, 3.3))[at]
 
 
 def kernel(

time: 30.6 us -> 30 us (0.980)
  Pallas kernels: 29.7 us -> 29.1 us
    pallas_call x1, Pallas kernels: 29.7 us -> 29.1 us  [per_device(): pl.pallas_call(functools.partial(kernel, n, chunks, orbits), out_shape=ja...]
where the time goes in v7:
time: 30 us; the launch traced here: 29.8 us
  Pallas kernels  29.1 us (97%)
  local copies, waits for them, and re-layouts  0.71 us (2%)
    pallas_call x1, Pallas kernels, per_device(): pl.pallas_call(functools.partial(kernel, n, chunks, orbits), out_shape=ja...  29.1 us
    unnamed x1, local copies, waits for them, and re-layouts  0.71 us

profile of v7, /device:TPU:0, one launch (start us, length us, event | category | flops | bytes accessed | tf_op | source)
XLA Modules:
  0.0 29.8 jit_solution(1900555149621389954)
XLA Ops:
  0.0 29.1 %shard_map.37 = f32[512,128]{1,0:T(8,128)S(1)} custom-call(f32[512,128]{1,0:T(8,128)} %bitcast.13, f32[512,128]{1,0:T(8,128)} %bitcast.14, f32[512,128]{1,0:T(8,128)} %bitcast.15), custom_call_target="tpu_custom_call" | custom-call | tf_op jit(solution)/shard_map/pallas_call | solution.py:261
  29.1 0.7 %copy.7 = f32[16,16,2,128]{3,2,1,0:T(2,128)} copy(f32[16,16,2,128]{3,2,1,0:T(2,128)S(1)} %bitcast.12) | data formatting | bytes 524288

commit v8 on v7

--- a/solution.py
+++ b/solution.py
@@ -9,7 +9,7 @@
 
 ITERS = 2
 STEP_WEIGHT = 0.5
-MOST_CHUNKS = 4
+MOST_CHUNKS = 2
 VMEM_LIMIT = 54784 * 1024
 MESH = pl.DeviceIdType.MESH
 

time: 30 us -> 31.3 us (1.043)
  the two profiles are of different devices: /device:TPU:0 before, /device:TPU:6 now
where the time goes in v8:
time: 31.3 us; the launch traced here: 31.1 us
  Pallas kernels  30.4 us (97%)
  local copies, waits for them, and re-layouts  0.71 us (2%)
    pallas_call x1, Pallas kernels, per_device(): pl.pallas_call(functools.partial(kernel, n, chunks, orbits), out_shape=ja...  30.4 us
    unnamed x1, local copies, waits for them, and re-layouts  0.71 us

profile of v8, /device:TPU:6, one launch (start us, length us, event | category | flops | bytes accessed | tf_op | source)
XLA Modules:
  0.0 31.1 jit_solution(12674898812470151881)
XLA Ops:
  0.0 30.4 %shard_map.37 = f32[512,128]{1,0:T(8,128)S(1)} custom-call(f32[512,128]{1,0:T(8,128)} %bitcast.13, f32[512,128]{1,0:T(8,128)} %bitcast.14, f32[512,128]{1,0:T(8,128)} %bitcast.15), custom_call_target="tpu_custom_call" | custom-call | tf_op jit(solution)/shard_map/pallas_call | solution.py:261
  30.4 0.7 %copy.7 = f32[16,16,2,128]{3,2,1,0:T(2,128)} copy(f32[16,16,2,128]{3,2,1,0:T(2,128)S(1)} %bitcast.12) | data formatting | bytes 524288

commit v9 on v7

--- a/solution.py
+++ b/solution.py
@@ -51,7 +51,7 @@
     if at == 3:
         return 8.3 * (it + 1) + 5.2 / chunks * h
     start = 8.3 * it + (5.2 if it else 2.8) / chunks * h
-    return start + ((0.0, 1.65, 3.85) if it else (0.0, 1.3, 3.3))[at]
+    return start + ((0.0, 1.25, 3.5) if it else (0.0, 1.3, 3.3))[at]
 
 
 def kernel(
@@ -195,7 +195,7 @@
             value = value + rs_in[it, h, d]
         total[it, h] = value
 
-        for d in range(1, n):
+        for d in sorted(range(1, n), key=lambda d: abs(2 * d - n)):
             done_copy(it, h, d).start()
 
         @pl.when(chip != plane)

time: 30 us -> 29.7 us (0.990)
  Pallas kernels: 29.1 us -> 28.8 us
    pallas_call x1, Pallas kernels: 29.1 us -> 28.8 us  [per_device(): pl.pallas_call(functools.partial(kernel, n, chunks, orbits), out_shape=ja...]
where the time goes in v9:
time: 29.7 us; the launch traced here: 29.5 us
  Pallas kernels  28.8 us (97%)
  local copies, waits for them, and re-layouts  0.71 us (2%)
    pallas_call x1, Pallas kernels, per_device(): pl.pallas_call(functools.partial(kernel, n, chunks, orbits), out_shape=ja...  28.8 us
    unnamed x1, local copies, waits for them, and re-layouts  0.71 us

profile of v9, /device:TPU:0, one launch (start us, length us, event | category | flops | bytes accessed | tf_op | source)
XLA Modules:
  0.0 29.5 jit_solution(9671912614819120407)
XLA Ops:
  0.0 28.8 %shard_map.37 = f32[512,128]{1,0:T(8,128)S(1)} custom-call(f32[512,128]{1,0:T(8,128)} %bitcast.13, f32[512,128]{1,0:T(8,128)} %bitcast.14, f32[512,128]{1,0:T(8,128)} %bitcast.15), custom_call_target="tpu_custom_call" | custom-call | tf_op jit(solution)/shard_map/pallas_call | solution.py:261
  28.8 0.7 %copy.7 = f32[16,16,2,128]{3,2,1,0:T(2,128)} copy(f32[16,16,2,128]{3,2,1,0:T(2,128)S(1)} %bitcast.12) | data formatting | bytes 524288

commit v10 on v9

--- a/solution.py
+++ b/solution.py
@@ -96,7 +96,7 @@
 
     def prepare(side):
         at = 0
-        for history in (green_ref, field_ref):
+        for history in (field_ref, green_ref):
             parts = []
             for part in range(2):
                 halves = [history[pl.ds(2 * half + part, depth, stride=4), :] for half in range(2)]
@@ -163,7 +163,7 @@
         ]
         sigma_re = jnp.concatenate([s[0] for s in sigmas], axis=0)
         sigma_im = jnp.concatenate([s[1] for s in sigmas], axis=0)
-        high, low = split(jnp.concatenate([sigma_re, sigma_im, real_part, imag_part], axis=1))
+        high, low = split(jnp.concatenate([real_part, imag_part, sigma_re, sigma_im], axis=1))
         both = jnp.concatenate([high, low], axis=0)
         for side, store in enumerate((pair_out.at[it], own)):
             if it == 0 and h == 0:

time: 29.7 us -> 29.4 us (0.990)
  Pallas kernels: 28.8 us -> 28.5 us
where the time goes in v10:
time: 29.4 us; the launch traced here: 29.2 us
  Pallas kernels  28.5 us (97%)
  local copies, waits for them, and re-layouts  0.71 us (2%)
    pallas_call x1, Pallas kernels, per_device(): pl.pallas_call(functools.partial(kernel, n, chunks, orbits), out_shape=ja...  28.5 us
    unnamed x1, local copies, waits for them, and re-layouts  0.71 us

profile of v10, /device:TPU:0, one launch (start us, length us, event | category | flops | bytes accessed | tf_op | source)
XLA Modules:
  0.0 29.2 jit_solution(14731138358268656400)
XLA Ops:
  0.0 28.5 %shard_map.37 = f32[512,128]{1,0:T(8,128)S(1)} custom-call(f32[512,128]{1,0:T(8,128)} %bitcast.13, f32[512,128]{1,0:T(8,128)} %bitcast.14, f32[512,128]{1,0:T(8,128)} %bitcast.15), custom_call_target="tpu_custom_call" | custom-call | tf_op jit(solution)/shard_map/pallas_call | solution.py:261
  28.5 0.7 %copy.7 = f32[16,16,2,128]{3,2,1,0:T(2,128)} copy(f32[16,16,2,128]{3,2,1,0:T(2,128)S(1)} %bitcast.12) | data formatting | bytes 524288
